TPU v7x, 512 devices: a whole 4x4x16 slice. The times are simulated.
512 devices in a mesh: seq: 64 (over y, z), head: 8 (over x, core).
Axes of the slice: x: 4, y: 4, z: 16, core: 2. Of those that a mesh axis runs over, the one named last changes fastest.
Arguments:
- queries: bfloat16 [8192, 4096], P(('seq', 'head')), may hold values from -16 to 16
- keys: bfloat16 [8192, 4096], P(('seq', 'head')), may hold values from -16 to 16
- values: bfloat16 [8192, 4096], P(('seq', 'head')), may hold values from -6 to 6
- out_grad: bfloat16 [8192, 4096], P(('seq', 'head')), may hold values from -6 to 6
Outputs:
- attended: bfloat16 [8192, 4096], P(('seq', 'head'))
- query_grad: bfloat16 [8192, 4096], P(('seq', 'head'))
- key_grad: bfloat16 [8192, 4096], P(('seq', 'head'))
- value_gradient_array: bfloat16 [8192, 4096], P(('seq', 'head'))
All inputs are finite; a program needn't handle non-finite values.
Results may differ from a plain program's by a relative error of at most 0.034.
The roundings to bfloat16 on the way count: a program that leaves them out, or rounds other values in their place, can miss the bound.
Values may be sent and summed in bfloat16 or wider, within the bound.
A program may use at most 64 MiB of HBM per device.

v0:
```python
import jax
import jax.numpy as jnp
from jax import lax
from jax.sharding import PartitionSpec as P

HD = 128
M = 256
PINV_ITERS = 6


precise_setting = lax.Precision.HIGHEST


def newton_inverse(matrix):
    identity = jnp.eye(matrix.shape[0], dtype=matrix.dtype)
    factor = lax.stop_gradient(1.0 / jnp.max(jnp.sum(matrix, axis=0)))
    iterate = matrix.T * factor
    for sweep_index in range(PINV_ITERS):
        product = jnp.matmul(matrix, iterate, precision=precise_setting)
        inner_term = jnp.matmul(product, 7.0 * identity - product, precision=precise_setting)
        inner_term = jnp.matmul(product, 15.0 * identity - inner_term, precision=precise_setting)
        iterate = 0.25 * jnp.matmul(
            iterate, 13.0 * identity - inner_term, precision=precise_setting
        )
    return iterate


def share_heads(own_matrix, head_count):
    seq_index = lax.axis_index("seq")
    slot_mask = (jnp.arange(head_count, dtype=jnp.int32) == seq_index).astype(jnp.float32)
    return lax.psum(slot_mask[:, None, None] * own_matrix[None], "seq")


def body(queries, keys, values, out_grad):
    query_rows, key_rows, value_rows, grad_rows = (
        lax.all_to_all(queries, "head", split_axis=1, concat_axis=0, tiled=True),
        lax.all_to_all(keys, "head", split_axis=1, concat_axis=0, tiled=True),
        lax.all_to_all(values, "head", split_axis=1, concat_axis=0, tiled=True),
        lax.all_to_all(out_grad, "head", split_axis=1, concat_axis=0, tiled=True),
    )
    tok_rows = query_rows.shape[0]
    head_count = query_rows.shape[1] // HD
    local_marks = M // lax.axis_size("seq")
    segment_len = tok_rows // local_marks
    score_scale = HD ** (-0.5)
    seq_index = lax.axis_index("seq")

    def landmark(matrix):
        summed = jnp.sum(
            matrix.reshape(local_marks, segment_len, matrix.shape[1]), axis=1, dtype=jnp.float32
        )
        return (summed / segment_len).astype(jnp.bfloat16)

    mark_queries, mark_keys = (
        lax.all_gather(landmark(query_rows), "seq", axis=0, tiled=True),
        lax.all_gather(landmark(key_rows), "seq", axis=0, tiled=True),
    )
    query_per_head = query_rows.reshape(tok_rows, head_count, HD)
    key_per_head = key_rows.reshape(tok_rows, head_count, HD)
    value_per_head = value_rows.reshape(tok_rows, head_count, HD)
    gradient_per_head = grad_rows.reshape(tok_rows, head_count, HD)
    landmark_query_heads = mark_queries.reshape(M, head_count, HD)
    landmark_key_heads = mark_keys.reshape(M, head_count, HD)
    key_score = (
        jnp.einsum(
            "pcv,gcv->cpg", landmark_query_heads, key_per_head, preferred_element_type=jnp.float32
        )
        * score_scale
    )
    key_max = lax.pmax(jnp.max(key_score, axis=-1), "seq")
    key_exp = jnp.exp(key_score - key_max[..., None])
    partial_num = jnp.einsum(
        "akq,qay->aky",
        key_exp.astype(jnp.bfloat16),
        value_per_head,
        preferred_element_type=jnp.float32,
    )
    key_total, numerator = lax.psum((jnp.sum(key_exp, axis=-1), partial_num), "seq")
    landmark_value_rows = numerator / key_total[..., None]
    token_prob = jax.nn.softmax(
        jnp.einsum(
            "jti,cti->tjc", query_per_head, landmark_key_heads, preferred_element_type=jnp.float32
        )
        * score_scale,
        axis=-1,
    )
    token_probability_lowered = token_prob.astype(jnp.bfloat16)
    mark_prob = jax.nn.softmax(
        jnp.einsum(
            "jou,iou->oji",
            landmark_query_heads,
            landmark_key_heads,
            preferred_element_type=jnp.float32,
        )
        * score_scale,
        axis=-1,
    )
    own_head = seq_index % head_count
    own_mark = lax.dynamic_index_in_dim(mark_prob, own_head, 0, keepdims=False)
    own_inverse, pull_back = jax.vjp(newton_inverse, own_mark)
    pseudo_inverse_matrix = share_heads(own_inverse, head_count)
    mixing_matrix = jnp.einsum(
        "jvy,jys->jvs", pseudo_inverse_matrix, landmark_value_rows, precision=precise_setting
    )
    mixing_matrix_lowered = mixing_matrix.astype(jnp.bfloat16)
    attended = jnp.einsum(
        "yvo,yor->vyr",
        token_probability_lowered,
        mixing_matrix_lowered,
        preferred_element_type=jnp.float32,
    ).astype(jnp.bfloat16)
    token_grad = jnp.einsum(
        "fag,aog->afo", gradient_per_head, mixing_matrix_lowered, preferred_element_type=jnp.float32
    )
    partial_mix = jnp.einsum(
        "klz,lkr->kzr",
        token_probability_lowered,
        gradient_per_head,
        preferred_element_type=jnp.float32,
    )
    mixing_matrix_gradient = lax.psum(partial_mix, "seq")
    token_score_gradient = (
        token_prob * (token_grad - jnp.sum(token_grad * token_prob, axis=-1, keepdims=True))
    ).astype(jnp.bfloat16)
    direct_qgrad = (
        jnp.einsum(
            "ufg,guc->fuc",
            token_score_gradient,
            landmark_key_heads,
            preferred_element_type=jnp.float32,
        )
        * score_scale
    )
    mark_kgrad_f = (
        jnp.einsum(
            "xgi,gxy->ixy", token_score_gradient, query_per_head, preferred_element_type=jnp.float32
        )
        * score_scale
    )
    pseudo_inverse_gradient = jnp.einsum(
        "ktu,kyu->kty", mixing_matrix_gradient, landmark_value_rows, precision=precise_setting
    )
    landmark_value_gradient = jnp.einsum(
        "lrb,lrz->lbz", pseudo_inverse_matrix, mixing_matrix_gradient, precision=precise_setting
    )
    own_igrad = lax.dynamic_index_in_dim(pseudo_inverse_gradient, own_head, 0, keepdims=False)
    (own_mgrad,) = pull_back(own_igrad)
    mark_grad = share_heads(own_mgrad, head_count)
    mark_sgrad = mark_prob * (mark_grad - jnp.sum(mark_grad * mark_prob, axis=-1, keepdims=True))
    first_mark = seq_index * local_marks
    score_gradient_rows = lax.dynamic_slice_in_dim(mark_sgrad, first_mark, local_marks, 1)
    score_gradient_columns = lax.dynamic_slice_in_dim(mark_sgrad, first_mark, local_marks, 2)
    own_qgrad_a = (
        jnp.einsum(
            "txs,ste->xte",
            score_gradient_rows,
            landmark_key_heads.astype(jnp.float32),
            precision=precise_setting,
        )
        * score_scale
    )
    own_kgrad_a = (
        jnp.einsum(
            "eaj,aev->jev",
            score_gradient_columns,
            landmark_query_heads.astype(jnp.float32),
            precision=precise_setting,
        )
        * score_scale
    )
    landmark_value_lowered = landmark_value_gradient.astype(jnp.bfloat16)
    key_prob = key_exp / key_total[..., None]
    key_probability_lowered = key_prob.astype(jnp.bfloat16)
    value_gradient_array = jnp.einsum(
        "zct,zcj->tzj",
        key_probability_lowered,
        landmark_value_lowered,
        preferred_element_type=jnp.float32,
    )
    key_direct_gradient = jnp.einsum(
        "exb,geb->exg", landmark_value_lowered, value_per_head, preferred_element_type=jnp.float32
    )
    row_total = lax.psum(jnp.sum(key_prob * key_direct_gradient, axis=-1), "seq")
    key_score_gradient = (key_prob * (key_direct_gradient - row_total[..., None])).astype(
        jnp.bfloat16
    )
    direct_kgrad = (
        jnp.einsum(
            "pbo,bpx->opx",
            key_score_gradient,
            landmark_query_heads,
            preferred_element_type=jnp.float32,
        )
        * score_scale
    )
    mark_qgrad_b = (
        jnp.einsum(
            "cbj,jcp->bcp", key_score_gradient, key_per_head, preferred_element_type=jnp.float32
        )
        * score_scale
    )
    own_kgrad_f, own_qgrad_b = (
        lax.psum_scatter(mark_kgrad_f, "seq", scatter_dimension=0, tiled=True),
        lax.psum_scatter(mark_qgrad_b, "seq", scatter_dimension=0, tiled=True),
    )
    mark_qtotal = (own_qgrad_a + own_qgrad_b) / segment_len
    mark_ktotal = (own_kgrad_a + own_kgrad_f) / segment_len
    query_grad = (
        direct_qgrad.reshape(local_marks, segment_len, head_count, HD) + mark_qtotal[:, None]
    )
    key_grad = direct_kgrad.reshape(local_marks, segment_len, head_count, HD) + mark_ktotal[:, None]
    width = head_count * HD
    results = (
        attended.reshape(tok_rows, width),
        query_grad.astype(jnp.bfloat16).reshape(tok_rows, width),
        key_grad.astype(jnp.bfloat16).reshape(tok_rows, width),
        value_gradient_array.astype(jnp.bfloat16).reshape(tok_rows, width),
    )
    attended_out, query_out, key_out, value_out = (
        lax.all_to_all(results[0], "head", split_axis=0, concat_axis=1, tiled=True),
        lax.all_to_all(results[1], "head", split_axis=0, concat_axis=1, tiled=True),
        lax.all_to_all(results[2], "head", split_axis=0, concat_axis=1, tiled=True),
        lax.all_to_all(results[3], "head", split_axis=0, concat_axis=1, tiled=True),
    )
    return (attended_out, query_out, key_out, value_out)


def solution(mesh):
    return jax.shard_map(
        body,
        mesh=mesh,
        in_specs=(
            P(("seq", "head"), None),
            P(("seq", "head"), None),
            P(("seq", "head"), None),
            P(("seq", "head"), None),
        ),
        out_specs=(
            P(("seq", "head"), None),
            P(("seq", "head"), None),
            P(("seq", "head"), None),
            P(("seq", "head"), None),
        ),
        check_vma=False,
    )
```

profile of v0, /device:TPU:1, one launch (start us, length us, event | category | flops | bytes accessed | tf_op | source)
XLA Modules:
  0.0 1146.3 jit_solution(11888160987268873308)
XLA Ops:
  8.7 10.3 all-to-all-start.1
  21.6 2.7 all-to-all-done.1
  24.3 4.1 all-to-all-start
  28.6 65.6 %all-gather.1 = bf16[64,4,512]{2,1,0:T(4,128)(2,1)S(1)} all-gather(bf16[1,4,512]{2,1,0:T(4,128)(2,1)S(1)} %fusion.122), channel_id=1, replica_groups=mesh['seq'=64,'head'=8] {'seq'}, dimensions={0}, use_global_device_ids=true | all-gather | bytes 266240 | tf_op jit(solution)/shard_map/all_gather | solution.py:56
  94.3 23.8 %all-to-all-start.2 = ((bf16[16,8,512]{2,0,1:T(8,128)(2,1)}), bf16[16,8,512]{2,0,1:T(8,128)(2,1)}, u32[]{:S(2)}, u32[]{:S(2)}) async-start(bf16[16,8,512]{2,0,1:T(8,128)(2,1)} %bitcast.259), calls=%async_computation.2 | async-start | bytes 262144 | tf_op jit(solution)/shard_map/all_to_all | solution.py:38
  118.2 62.2 %all-gather = bf16[64,4,512]{2,1,0:T(4,128)(2,1)S(1)} all-gather(bf16[1,4,512]{2,1,0:T(4,128)(2,1)S(1)} %fusion.121), channel_id=1, replica_groups=mesh['seq'=64,'head'=8] {'seq'}, dimensions={0}, use_global_device_ids=true | all-gather | bytes 266240 | tf_op jit(solution)/shard_map/all_gather | solution.py:55
  201.5 23.4 %all-to-all-start.4 = ((bf16[16,8,512]{2,0,1:T(8,128)(2,1)}), bf16[16,8,512]{2,0,1:T(8,128)(2,1)}, u32[]{:S(2)}, u32[]{:S(2)}) async-start(bf16[16,8,512]{2,0,1:T(8,128)(2,1)} %bitcast.266), calls=%async_computation.4 | async-start | bytes 262144 | tf_op jit(solution)/shard_map/all_to_all | solution.py:39
  224.9 2.1 convolution_multiply_fusion.7
  230.4 113.0 %pmax.7 = f32[4,256]{1,0:T(4,128)S(1)} all-reduce(f32[4,256]{1,0:T(4,128)S(1)} %get-tuple-element.14), channel_id=1, replica_groups=mesh['seq'=64,'head'=8] {'seq'}, use_global_device_ids=true, to_apply=%region_10.0 | all-reduce | flops 1024 | bytes 8192 | tf_op jit(solution)/shard_map/pmax | solution.py:70
  346.6 2.1 fusion.189
  350.8 3.0 fusion.72
  355.9 111.0 %psum.44 = f32[4,256]{1,0:T(4,128)S(1)} all-reduce(f32[4,256]{1,0:T(4,128)S(1)} %fusion.34), channel_id=1, replica_groups=mesh['seq'=64,'head'=8] {'seq'}, use_global_device_ids=true, to_apply=%region_13.14 | all-reduce | flops 1024 | bytes 8192 | tf_op jit(solution)/shard_map/psum | solution.py:78
  466.9 174.3 %all-reduce.9.cloned.1.call-done = (f32[4,256,256]{1,2,0:T(8,128)}, f32[4,256,128]{1,2,0:T(8,128)}, f32[4,256,128]{2,1,0:T(8,128)}) async-done(((f32[4,256,256]{1,2,0:T(8,128)}, f32[4,256,128]{1,2,0:T(8,128)}, f32[4,256,128]{2,1,0:T(8,128)}), (f32[4,256,256]{1,2,0:T(8,128)}, f32[4,256,128]{1,2,0:T(8,128)}, f32[4,256,128]{2,1,0:T(8,128)})) %all-reduce.9.cloned.1.call-update) | async-done | bytes 2097168 | tf_op jit(solution)/shard_map/psum | solution.py:31
  641.2 2.2 fusion.61
  672.0 2.6 convolution_convert_fusion.1
  682.4 113.2 %psum.47 = f32[4,256]{1,0:T(4,128)S(1)} all-reduce(f32[4,256]{1,0:T(4,128)S(1)} %get-tuple-element.20), channel_id=1, replica_groups=mesh['seq'=64,'head'=8] {'seq'}, use_global_device_ids=true, to_apply=%region_21.22 | all-reduce | flops 1024 | bytes 8192 | tf_op jit(solution)/shard_map/psum | solution.py:183
  804.5 42.2 %all-to-all-start.3 = ((bf16[8,16,512]{2,1,0:T(8,128)(2,1)}), bf16[8,16,512]{2,1,0:T(8,128)(2,1)S(1)}, u32[]{:S(2)}, u32[]{:S(2)}) async-start(bf16[8,16,512]{2,1,0:T(8,128)(2,1)} %all_to_all.109), calls=%async_computation.3 | async-start | bytes 262144 | tf_op jit(solution)/shard_map/all_to_all | solution.py:220
  850.6 245.0 %all-reduce.7.cloned.1.call-done = (f32[4,256,256]{1,2,0:T(8,128)}, f32[256,4,128]{2,1,0:T(4,128)}, f32[256,4,128]{2,1,0:T(4,128)}) async-done(((f32[4,256,256]{1,2,0:T(8,128)}, f32[256,4,128]{2,1,0:T(4,128)}, f32[256,4,128]{2,1,0:T(4,128)}), (f32[4,256,256]{1,2,0:T(8,128)}, f32[256,4,128]{2,1,0:T(4,128)}, f32[256,4,128]{2,1,0:T(4,128)})) %all-reduce.7.cloned.1.call-update) | async-done | bytes 2097168 | tf_op jit(solution)/shard_map/psum | solution.py:31
  1099.7 14.5 %all-to-all-start.7 = ((bf16[8,16,512]{2,1,0:T(8,128)(2,1)}), bf16[8,16,512]{2,1,0:T(8,128)(2,1)S(1)}, u32[]{:S(2)}, u32[]{:S(2)}) async-start(bf16[8,16,512]{2,1,0:T(8,128)(2,1)} %all_to_all.122), calls=%async_computation.7 | async-start | bytes 262144 | tf_op jit(solution)/shard_map/all_to_all | solution.py:223
  1114.4 5.0 all-to-all-done.7
  1119.5 4.1 all-to-all-start.5
  1124.3 4.6 all-to-all-done.5
  1128.9 4.1 all-to-all-start.6
  1135.0 3.3 all-to-all-done.6
  (271 shorter events, 90.7 us)
Async XLA Ops:
  8.7 10.3 copy-start.52
  8.7 15.6 %all-to-all-start.1 = ((bf16[16,8,512]{2,0,1:T(8,128)(2,1)}), bf16[16,8,512]{2,0,1:T(8,128)(2,1)S(1)}, u32[]{:S(2)}, u32[]{:S(2)}) async-start(bf16[16,8,512]{2,0,1:T(8,128)(2,1)} %bitcast.260), calls=%async_computation.1 | async-start | bytes 262144 | tf_op jit(solution)/shard_map/all_to_all | solution.py:37
  21.6 327.1 %copy-start.58 = (f32[4]{0:T(128)}, f32[4]{0:T(128)S(1)}, u32[]{:S(2)}) copy-start(f32[4]{0:T(128)S(1)} %compare_convert_fusion) | copy-start | bytes 52
  24.3 4.1 copy-start.41
  24.3 70.0 %all-to-all-start = ((bf16[16,8,512]{2,0,1:T(8,128)(2,1)}), bf16[16,8,512]{2,0,1:T(8,128)(2,1)S(1)}, u32[]{:S(2)}, u32[]{:S(2)}) async-start(bf16[16,8,512]{2,0,1:T(8,128)(2,1)} %bitcast.261), calls=%async_computation | async-start | bytes 262144 | tf_op jit(solution)/shard_map/all_to_all | solution.py:36
  94.3 86.3 %copy-start.38 = (bf16[256,4,128]{2,1,0:T(4,128)(2,1)}, bf16[256,4,128]{2,1,0:T(4,128)(2,1)S(1)}, u32[]{:S(2)}) copy-start(bf16[256,4,128]{2,1,0:T(4,128)(2,1)S(1)} %reshape.103) | copy-start | bytes 786436
  94.3 86.1 %copy-start.43 = (bf16[16,8,512]{2,0,1:T(8,128)(2,1)}, bf16[16,8,512]{2,0,1:T(8,128)(2,1)S(1)}, u32[]{:S(2)}) copy-start(bf16[16,8,512]{2,0,1:T(8,128)(2,1)S(1)} %all-to-all-done) | copy-start | bytes 393220
  94.3 107.1 %all-to-all-start.2 = ((bf16[16,8,512]{2,0,1:T(8,128)(2,1)}), bf16[16,8,512]{2,0,1:T(8,128)(2,1)}, u32[]{:S(2)}, u32[]{:S(2)}) async-start(bf16[16,8,512]{2,0,1:T(8,128)(2,1)} %bitcast.259), calls=%async_computation.2 | async-start | bytes 262144 | tf_op jit(solution)/shard_map/all_to_all | solution.py:38
  181.6 3.4 copy-start.10
  185.7 2.1 copy-start.8
  188.6 2.1 copy-start
  191.4 2.1 copy-start.2
  194.2 2.1 copy-start.4
  201.5 141.9 %all-to-all-start.4 = ((bf16[16,8,512]{2,0,1:T(8,128)(2,1)}), bf16[16,8,512]{2,0,1:T(8,128)(2,1)}, u32[]{:S(2)}, u32[]{:S(2)}) async-start(bf16[16,8,512]{2,0,1:T(8,128)(2,1)} %bitcast.266), calls=%async_computation.4 | async-start | bytes 262144 | tf_op jit(solution)/shard_map/all_to_all | solution.py:39
  224.9 416.3 %all-reduce.9.cloned.1.call-start = ((), (), s32[]{:S(2)}) async-start(), calls=%async_computation.9 | async-start | bytes 4194304 | tf_op jit(solution)/shard_map/psum | solution.py:31
  348.7 2.1 copy-start.56
  355.7 739.9 %all-reduce.7.cloned.1.call-start = ((), (), s32[]{:S(2)}) async-start(), calls=%async_computation.8 | async-start | bytes 4194304 | tf_op jit(solution)/shard_map/psum | solution.py:31
  641.2 2.3 copy-start.37
  672.0 2.6 copy-start.40
  800.5 2.0 copy-start.60
  804.5 295.2 %all-to-all-start.3 = ((bf16[8,16,512]{2,1,0:T(8,128)(2,1)}), bf16[8,16,512]{2,1,0:T(8,128)(2,1)S(1)}, u32[]{:S(2)}, u32[]{:S(2)}) async-start(bf16[8,16,512]{2,1,0:T(8,128)(2,1)} %all_to_all.109), calls=%async_computation.3 | async-start | bytes 262144 | tf_op jit(solution)/shard_map/all_to_all | solution.py:220
  1099.7 19.8 %all-to-all-start.7 = ((bf16[8,16,512]{2,1,0:T(8,128)(2,1)}), bf16[8,16,512]{2,1,0:T(8,128)(2,1)S(1)}, u32[]{:S(2)}, u32[]{:S(2)}) async-start(bf16[8,16,512]{2,1,0:T(8,128)(2,1)} %all_to_all.122), calls=%async_computation.7 | async-start | bytes 262144 | tf_op jit(solution)/shard_map/all_to_all | solution.py:223
  1119.5 9.4 all-to-all-start.5
  1128.9 9.4 all-to-all-start.6
  (47 other events, 44.9 us)
Sparse Core Ops, SparseCore 0:
  355.9 285.2 all-reduce.8
  800.6 294.9 all-reduce.6
where the time goes:
time: 1160 us; the launch traced here: 1150 us
  blocking collectives  465 us (40%)
  waiting for transfers between devices  435 us (38%)
  starting transfers between devices  127 us (11%)
  matrix products  57.7 us (5%)
  local copies, waits for them, and re-layouts  37.3 us (3%)
  between operations  17 us (1%)
    psum x2, waiting for transfers between devices, share_heads(): return lax.psum(slot_mask[:, None, None] * own_matrix[None], 'seq')  419 us
    psum x1, blocking collectives, body(): lax.psum(jnp.sum(key_prob * key_direct_gradient, axis=-1), 'seq')  113 us
    pmax x1, blocking collectives, body(): key_max = lax.pmax(jnp.max(key_score, axis=-1), 'seq')  113 us
    psum x1, blocking collectives, body(): lax.psum((jnp.sum(key_exp, axis=-1), partial_num), 'seq')  111 us
    all_gather x1, blocking collectives, body(): lax.all_gather(landmark(key_rows), 'seq', axis=0, tiled=True)  65.6 us
    all_gather x1, blocking collectives, body(): lax.all_gather(landmark(query_rows), 'seq', axis=0, tiled=True)  62.2 us
    all_to_all x1, starting transfers between devices, body(): lax.all_to_all(results[0], 'head', split_axis=0, concat_axis=1, tiled=True)  42.2 us
    all_to_all x1, starting transfers between devices, body(): lax.all_to_all(values, 'head', split_axis=1, concat_axis=0, tiled=True)  23.8 us
  transfers between devices with their start and end apart: 10, of which 6 were waited for; matrix products, arithmetic and copies ran while one was open for 3% of the time, Pallas kernels for 0%

commit v1 on v0

v1 whole, which is shorter than its diff:
```python
import functools

import jax
import jax.numpy as jnp
from jax import lax
from jax.experimental import pallas as pl
from jax.experimental.pallas import tpu as pltpu
from jax.sharding import PartitionSpec as P

MESH = pl.DeviceIdType.MESH
F32, BF16 = jnp.float32, jnp.bfloat16

NZ = 16
PLANE = 32
HEADS = 8
ROWS = 16
HD = 128
D = PLANE * HD
TOK = PLANE * ROWS
SEG = 32
OWN = TOK // SEG
M = NZ * OWN
SLAB = HD // NZ
ITERS = 6
SCALE = HD ** (-0.5)

X_QK, X_VG, X_MARK, X_PART, X_SUM, X_AV, X_GRAD, X_OUT = range(8)


def dot(left, right):
    return lax.dot_general(left, right, (((1,), (0,)), ((), ())), preferred_element_type=F32)


def dot_nt(left, right):
    return lax.dot_general(left, right, (((1,), (1,)), ((), ())), preferred_element_type=F32)


def split(x):
    high = x.astype(BF16)
    return high, (x - high.astype(F32)).astype(BF16)


def mul(left, right, product=dot):
    return product(left[0], right[0]) + (product(left[0], right[1]) + product(left[1], right[0]))


def kernel(
    q_ref, k_ref, v_ref, g_ref, av_ref, qk_ref,
    qk_in, vg_in, qk, vg, mark_out, marks, part_out, parts, sum_out, sums, av_out, grad_out, grads, qk_out,
    prob, low, kexp, trans, direct, square, saved, load_sem, send_sem, recv_sem,
):
    seq, head = lax.axis_index("seq"), lax.axis_index("head")
    y, z = seq // NZ, seq % NZ
    me = y * HEADS + head

    def plane_peer(rank):
        return (rank // HEADS * NZ + z, rank % HEADS)

    def line_peer(rank):
        return (y * NZ + rank, head)

    loads = [
        pltpu.make_async_copy(source, target, load_sem.at[index])
        for index, (source, target) in enumerate(
            ((q_ref, qk_in.at[0]), (k_ref, qk_in.at[1]), (v_ref, vg_in.at[0]), (g_ref, vg_in.at[1]))
        )
    ]
    for load in loads:
        load.start()

    barrier = pltpu.get_barrier_semaphore()

    @pl.loop(1, PLANE)
    def _(step):
        pl.semaphore_signal(barrier, inc=1, device_id=plane_peer((me + step) % PLANE), device_id_type=MESH)

    @pl.loop(1, NZ)
    def _(step):
        pl.semaphore_signal(barrier, inc=1, device_id=line_peer((z + step) % NZ), device_id_type=MESH)

    pl.semaphore_wait(barrier, PLANE - 1 + NZ - 1)

    def send(source, target, index, peer):
        pltpu.make_async_remote_copy(
            src_ref=source, dst_ref=target, send_sem=send_sem.at[index], recv_sem=recv_sem.at[index],
            device_id=peer, device_id_type=MESH,
        ).start()

    def columns(rank):
        return pl.ds(pl.multiple_of(rank * HD, HD), HD)

    def rows(rank, count):
        return pl.ds(pl.multiple_of(rank * count, count), count)

    def scatter_heads(source, target, index):
        @pl.loop(1, PLANE)
        def _(step):
            peer = (me + step) % PLANE
            send(source.at[:, :, columns(peer)], target.at[:, rows(me, ROWS), :], index, plane_peer(peer))

        target[:, rows(me, ROWS), :] = source[:, :, columns(me)]

    def gather_heads(source, target, index):
        @pl.loop(1, PLANE)
        def _(step):
            peer = (me + step) % PLANE
            send(source.at[:, rows(peer, ROWS), :], target.at[:, :, columns(me)], index, plane_peer(peer))

        own = pltpu.make_async_copy(source.at[:, rows(me, ROWS), :], target.at[:, :, columns(me)], load_sem.at[0])
        own.start()
        own.wait()

    def over_line(source, target, index):
        @pl.loop(1, NZ)
        def _(step):
            peer = (z + step) % NZ
            send(source(peer), target.at[z], index, line_peer(peer))

    def arrived(span, index):
        pltpu.make_async_copy(span, span, recv_sem.at[index]).wait()

    def left(span, index):
        pltpu.make_async_copy(span, span, send_sem.at[index]).wait()

    loads[0].wait()
    loads[1].wait()
    scatter_heads(qk_in, qk, X_QK)
    loads[2].wait()
    loads[3].wait()
    scatter_heads(vg_in, vg, X_VG)
    plane_span = qk.at[:, pl.ds(0, TOK - ROWS), :]
    arrived(plane_span, X_QK)

    for index in range(2):
        summed = jnp.sum(qk[index].astype(F32).reshape(OWN, SEG, HD), axis=1)
        mark_out[index] = (summed * (1.0 / SEG)).astype(BF16)
    over_line(lambda peer: mark_out, marks, X_MARK)
    marks[z] = mark_out[...]
    for index in range(2):
        trans[index] = qk[index].T
    arrived(plane_span, X_VG)
    for index in range(2):
        trans[2 + index] = vg[index].T
    arrived(marks.at[pl.ds(0, NZ - 1)], X_MARK)
    mark_q = marks[:, 0].reshape(M, HD)
    mark_k = marks[:, 1].reshape(M, HD)

    scores = dot_nt(qk[0], mark_k)
    top = jnp.max(scores, axis=1, keepdims=True)
    exps = jnp.exp((scores - top) * SCALE)
    token_prob = exps * (1.0 / jnp.sum(exps, axis=1, keepdims=True))
    prob[...] = token_prob
    token_low = token_prob.astype(BF16)
    low[...] = token_low
    mixing_part = dot(trans[3], token_low)

    scores = dot_nt(qk[1], mark_q)
    key_top = jnp.max(scores, axis=0, keepdims=True)
    exps = jnp.exp((scores - key_top) * SCALE)
    kexp[...] = exps
    key_sum = jnp.sum(exps, axis=0, keepdims=True)
    value_part = dot(trans[2], exps.astype(BF16))
    part_out[:, 0:SLAB, :] = value_part.reshape(NZ, SLAB, M)
    part_out[:, SLAB : 2 * SLAB, :] = mixing_part.reshape(NZ, SLAB, M)
    stats = jnp.concatenate([jnp.broadcast_to(key_top, (4, M)), jnp.broadcast_to(key_sum, (4, M))], axis=0)
    part_out[:, 2 * SLAB : 3 * SLAB, :] = jnp.broadcast_to(stats[None], (NZ, SLAB, M))
    over_line(lambda peer: part_out.at[peer], parts, X_PART)
    parts[z] = part_out[z]

    scores = dot_nt(mark_q, mark_k)
    exps = jnp.exp((scores - jnp.max(scores, axis=1, keepdims=True)) * SCALE)
    mark_prob = exps * (1.0 / jnp.sum(exps, axis=1, keepdims=True))
    square[0] = mark_prob
    factor = 1.0 / jnp.max(jnp.sum(mark_prob, axis=0, keepdims=True))
    square[1] = mark_prob.T * factor

    def keep(step, slot, value):
        saved[step, slot], saved[step, slot + 1] = split(value)

    def kept(step, slot):
        return saved[step, slot], saved[step, slot + 1]

    mark_split = split(mark_prob)
    keep(ITERS, 8, mark_prob.T)

    @pl.loop(0, ITERS)
    def _(step):
        iterate = square[1]
        keep(step, 0, iterate)
        keep(step, 2, iterate.T)
        part = kept(step, 0)
        product = mul(split(square[0]), part)
        keep(step, 4, product)
        product_split = kept(step, 4)
        first = 7.0 * product - mul(product_split, product_split)
        keep(step, 6, first)
        second = 15.0 * product - mul(product_split, kept(step, 6))
        keep(step, 8, second)
        square[1] = 3.25 * iterate - 0.25 * mul(part, kept(step, 8))

    keep(ITERS, 0, square[1])

    arrived(parts.at[pl.ds(0, NZ - 1)], X_PART)
    tops = [parts[peer, 2 * SLAB : 2 * SLAB + 1, :] for peer in range(NZ)]
    highest = functools.reduce(jnp.maximum, tops)
    total, values, mixing_grad = 0.0, 0.0, 0.0
    for peer in range(NZ):
        weight = jnp.exp((tops[peer] - highest) * SCALE)
        total = total + weight * parts[peer, 2 * SLAB + 4 : 2 * SLAB + 5, :]
        values = values + weight * parts[peer, 0:SLAB, :]
        mixing_grad = mixing_grad + parts[peer, SLAB : 2 * SLAB, :]
    sum_out[0:SLAB, :] = values / total
    sum_out[SLAB : 2 * SLAB, :] = mixing_grad
    over_line(lambda peer: sum_out, sums, X_SUM)
    sums[z] = sum_out[...]
    key_prob = kexp[...] * (jnp.exp((key_top - highest) * SCALE) / total)
    kexp[...] = key_prob
    arrived(sums.at[pl.ds(0, NZ - 1)], X_SUM)
    values = sums[:, 0:SLAB, :].reshape(HD, M)
    mixing_grad = sums[:, SLAB : 2 * SLAB, :].reshape(HD, M)
    values_split, grad_split = split(values), split(mixing_grad)
    inverse = kept(ITERS, 0)
    mixing_low = mul(values_split, inverse, dot_nt).astype(BF16)
    lv_low = mul(grad_split, inverse).astype(BF16)
    square[1] = mul(split(mixing_grad.T), values_split)
    square[2] = jnp.zeros((M, M), F32)

    token_prob = prob[...]
    av_out[0] = dot_nt(low[...], mixing_low).astype(BF16)
    token_grad = dot(vg[1], mixing_low)
    dots = jnp.sum(token_grad * token_prob, axis=1, keepdims=True)
    token_sgrad = (token_prob * (token_grad - dots)).astype(BF16)
    direct[0] = dot(token_sgrad, mark_k) * SCALE
    grad_out[0] = (dot(trans[0], token_sgrad) * SCALE).T
    key_prob = kexp[...]
    av_out[1] = dot_nt(key_prob.astype(BF16), lv_low).astype(BF16)
    row_total = jnp.sum(lv_low.astype(F32) * values, axis=0, keepdims=True)
    key_dgrad = dot(vg[0], lv_low)
    key_sgrad = (key_prob * (key_dgrad - row_total)).astype(BF16)
    direct[1] = dot(key_sgrad, mark_q) * SCALE
    grad_out[1] = (dot(trans[1], key_sgrad) * SCALE).T
    over_line(lambda peer: grad_out.at[:, rows(peer, OWN), :], grads, X_GRAD)
    grads[z] = grad_out[:, rows(z, OWN), :]
    gather_heads(av_out, av_ref, X_AV)

    @pl.loop(0, ITERS)
    def _(back):
        step = ITERS - 1 - back
        out_grad = square[1]
        out_split = split(out_grad)
        second_grad = -0.25 * mul(kept(step, 2), out_split)
        iterate_grad = 3.25 * out_grad - 0.25 * mul(out_split, kept(step, 8))
        second_split = split(second_grad)
        product_split = kept(step, 4)
        product_grad = 15.0 * second_grad - mul(second_split, kept(step, 6))
        first_grad = -mul(product_split, second_split)
        first_split = split(first_grad)
        product_grad = product_grad + 7.0 * first_grad
        product_grad = product_grad - (mul(first_split, product_split) + mul(product_split, first_split))
        product_grad_split = split(product_grad)
        square[2] += mul(product_grad_split, kept(step, 0), dot_nt)
        square[1] = iterate_grad + mul(kept(ITERS, 8), product_grad_split)

    mark_grad = square[2] + square[1].T * factor
    mark_prob = square[0]
    mark_sgrad = mark_prob * (mark_grad - jnp.sum(mark_grad * mark_prob, axis=1, keepdims=True))
    square[1] = mark_sgrad
    square[2] = mark_sgrad.T
    arrived(grads.at[pl.ds(0, NZ - 1)], X_GRAD)
    from_query, from_key = split(square[1, rows(z, OWN), :]), split(square[2, rows(z, OWN), :])
    query_marks = (dot(from_query[0], mark_k) + dot(from_query[1], mark_k)) * SCALE
    key_marks = (dot(from_key[0], mark_q) + dot(from_key[1], mark_q)) * SCALE
    for peer in range(NZ):
        query_marks = query_marks + grads[peer, 1]
        key_marks = key_marks + grads[peer, 0]
    for index, total in ((0, query_marks), (1, key_marks)):
        spread = direct[index].reshape(OWN, SEG, HD) + (total * (1.0 / SEG))[:, None, :]
        qk_out[index] = spread.reshape(TOK, HD).astype(BF16)
    gather_heads(qk_out, qk_ref, X_OUT)

    out_span = av_ref.at[:, :, pl.ds(0, D - HD)]
    arrived(out_span, X_AV)
    arrived(out_span, X_OUT)
    for index in (X_QK, X_VG, X_AV, X_OUT):
        left(plane_span, index)
    left(marks.at[pl.ds(0, NZ - 1)], X_MARK)
    left(parts.at[pl.ds(0, NZ - 1)], X_PART)
    left(sums.at[pl.ds(0, NZ - 1)], X_SUM)
    left(grads.at[pl.ds(0, NZ - 1)], X_GRAD)


def body(queries, keys, values, out_grad):
    pair = jax.ShapeDtypeStruct((2, ROWS, D), BF16)
    anywhere = pl.BlockSpec(memory_space=pl.ANY)
    av, qk = pl.pallas_call(
        kernel,
        out_shape=(pair, pair),
        in_specs=[anywhere] * 4,
        out_specs=(anywhere, anywhere),
        scratch_shapes=[
            pltpu.VMEM((2, ROWS, D), BF16),
            pltpu.VMEM((2, ROWS, D), BF16),
            pltpu.VMEM((2, TOK, HD), BF16),
            pltpu.VMEM((2, TOK, HD), BF16),
            pltpu.VMEM((2, OWN, HD), BF16),
            pltpu.VMEM((NZ, 2, OWN, HD), BF16),
            pltpu.VMEM((NZ, 3 * SLAB, M), F32),
            pltpu.VMEM((NZ, 3 * SLAB, M), F32),
            pltpu.VMEM((2 * SLAB, M), F32),
            pltpu.VMEM((NZ, 2 * SLAB, M), F32),
            pltpu.VMEM((2, TOK, HD), BF16),
            pltpu.VMEM((2, M, HD), F32),
            pltpu.VMEM((NZ, 2, OWN, HD), F32),
            pltpu.VMEM((2, TOK, HD), BF16),
            pltpu.VMEM((TOK, M), F32),
            pltpu.VMEM((TOK, M), BF16),
            pltpu.VMEM((TOK, M), F32),
            pltpu.VMEM((4, HD, TOK), BF16),
            pltpu.VMEM((2, TOK, HD), F32),
            pltpu.VMEM((3, M, M), F32),
            pltpu.VMEM((ITERS + 1, 10, M, M), BF16),
            pltpu.SemaphoreType.DMA((4,)),
            pltpu.SemaphoreType.DMA((8,)),
            pltpu.SemaphoreType.DMA((8,)),
        ],
        compiler_params=pltpu.CompilerParams(
            collective_id=0, has_side_effects=True, vmem_limit_bytes=48 * 1024 * 1024
        ),
    )(queries, keys, values, out_grad)
    return av[0], qk[0], qk[1], av[1]


def solution(mesh):
    spec = P(("seq", "head"), None)
    return jax.shard_map(body, mesh=mesh, in_specs=(spec,) * 4, out_specs=(spec,) * 4, check_vma=False)
```

time: 1160 us -> 97.2 us (0.08); the launches traced: 1150 us -> 97 us
  blocking collectives: 465 us -> 0 us
  waiting for transfers between devices: 435 us -> 0 us
  starting transfers between devices: 127 us -> 0 us
  Pallas kernels: 0 us -> 91.9 us
  matrix products: 57.7 us -> 0 us
  local copies, waits for them, and re-layouts: 37.3 us -> 4.4 us
  between operations: 17 us -> 0.65 us
    psum x2 -> x0, waiting for transfers between devices: 419 us -> none  [share_heads(): return lax.psum(slot_mask[:, None, None] * own_matrix[None], 'seq')]
    psum x2 -> x0, blocking collectives: 224 us -> none  [the longest x1 113 us: body(): lax.psum(jnp.sum(key_prob * key_direct_gradient, axis=-1), 'seq')]
    all_gather x2 -> x0, blocking collectives: 128 us -> none  [the longest x1 65.6 us: body(): lax.all_gather(landmark(key_rows), 'seq', axis=0, tiled=True)]
    all_to_all x8 -> x0, starting transfers between devices: 127 us -> none  [the longest x1 42.2 us: body(): lax.all_to_all(results[0], 'head', split_axis=0, concat_axis=1, tiled=True)]
    pmax x1 -> x0, blocking collectives: 113 us -> none  [body(): key_max = lax.pmax(jnp.max(key_score, axis=-1), 'seq')]
    pallas_call x0 -> x1, Pallas kernels: none -> 91.9 us  [body(): pl.pallas_call(kernel, out_shape=(pair, pair), in_specs=[anywhere] * 4, o...]
    dot_general x88 -> x0, matrix products: 55.1 us -> none  [the longest x18 10.3 us: newton_inverse(): jnp.matmul(iterate, 13.0 * identity - inner_term, precision=precise_setting)]
    all_to_all x8 -> x0, waiting for transfers between devices: 15.7 us -> none  [the longest x1 5.03 us: body(): lax.all_to_all(results[3], 'head', split_axis=0, concat_axis=1, tiled=True)]
  transfers between devices with their start and end apart: 10 -> 0, of which waited for: 6 -> 0; matrix products, arithmetic and copies ran while one was open for 3% -> 0% of each run, Pallas kernels for 0% -> 0%
where the time goes in v1:
time: 97.2 us; the launch traced here: 97 us
  Pallas kernels  91.9 us (95%)
  local copies, waits for them, and re-layouts  4.4 us (5%)
    pallas_call x1, Pallas kernels, body(): pl.pallas_call(kernel, out_shape=(pair, pair), in_specs=[anywhere] * 4, o...  91.9 us
    unnamed x8, local copies, waits for them, and re-layouts  3.61 us

profile of v1, /device:TPU:1, one launch (start us, length us, event | category | flops | bytes accessed | tf_op | source)
XLA Modules:
  0.0 97.0 jit_solution(8655244211790431883)
XLA Ops:
  0.6 0.0 copy-start
  0.6 0.9 copy-done
  1.5 0.0 copy-start.1
  1.5 0.9 copy-done.1
  2.4 0.0 copy-start.2
  2.4 0.9 copy-done.2
  3.3 0.0 copy-start.3
  3.3 0.9 copy-done.3
  4.3 91.9 %shard_map.75 = (bf16[2,16,4096]{2,1,0:T(8,128)(2,1)S(1)}, bf16[2,16,4096]{2,1,0:T(8,128)(2,1)S(1)}) custom-call(bf16[16,4096]{1,0:T(8,128)(2,1)S(1)} %copy-done, bf16[16,4096]{1,0:T(8,128)(2,1)S(1)} %copy-done.1, bf16[16,4096]{1,0:T(8,128)(2,1)S(1)} %copy-done.2, bf16[16,4096]{1,0:T(8,128)(2,1)S(1)} %copy-done.3), custom_call_target="tpu_custom_call" | custom-call | tf_op jit(solution)/shard_map/pallas_call | solution.py:295
  96.2 0.8 slice_bitcast_fusion
Async XLA Ops:
  0.6 0.9 copy-start
  1.5 0.9 copy-start.1
  2.4 0.9 copy-start.2
  3.3 0.9 copy-start.3

commit v2 on v1

--- a/solution.py
+++ b/solution.py
@@ -24,7 +24,19 @@
 ITERS = 6
 SCALE = HD ** (-0.5)
 
-X_QK, X_VG, X_MARK, X_PART, X_SUM, X_AV, X_GRAD, X_OUT = range(8)
+
+def away(step, size):
+    return min(step % size, -step % size)
+
+
+NY, NX = 4, 4
+PLANE_STEPS = sorted(
+    ((i, j, k) for i in range(NY) for j in range(NX) for k in range(2) if i or j or k),
+    key=lambda step: -away(step[0], NY) - away(step[1], NX),
+)
+LINE_STEPS = sorted(range(1, NZ), key=lambda step: -away(step, NZ))
+
+X_QK, X_VG, X_MARK, X_PART, X_SUM, X_AV, X_GRAD, X_OUT, X_STAT = range(9)
 
 
 def dot(left, right):
@@ -46,7 +58,7 @@
 
 def kernel(
     q_ref, k_ref, v_ref, g_ref, av_ref, qk_ref,
-    qk_in, vg_in, qk, vg, mark_out, marks, part_out, parts, sum_out, sums, av_out, grad_out, grads, qk_out,
+    qk_in, vg_in, qk, vg, mark_out, marks, part_out, parts, stat_out, stats, sum_out, sums, av_out, grad_out, grads, qk_out,
     prob, low, kexp, trans, direct, square, saved, load_sem, send_sem, recv_sem,
 ):
     seq, head = lax.axis_index("seq"), lax.axis_index("head")
@@ -92,18 +104,18 @@
     def rows(rank, count):
         return pl.ds(pl.multiple_of(rank * count, count), count)
 
+    def plane_ranks():
+        for i, j, k in PLANE_STEPS:
+            yield (y + i) % NY * HEADS + (head // 2 + j) % NX * 2 + (head + k) % 2
+
     def scatter_heads(source, target, index):
-        @pl.loop(1, PLANE)
-        def _(step):
-            peer = (me + step) % PLANE
+        for peer in plane_ranks():
             send(source.at[:, :, columns(peer)], target.at[:, rows(me, ROWS), :], index, plane_peer(peer))
 
         target[:, rows(me, ROWS), :] = source[:, :, columns(me)]
 
     def gather_heads(source, target, index):
-        @pl.loop(1, PLANE)
-        def _(step):
-            peer = (me + step) % PLANE
+        for peer in plane_ranks():
             send(source.at[:, rows(peer, ROWS), :], target.at[:, :, columns(me)], index, plane_peer(peer))
 
         own = pltpu.make_async_copy(source.at[:, rows(me, ROWS), :], target.at[:, :, columns(me)], load_sem.at[0])
@@ -111,8 +123,7 @@
         own.wait()
 
     def over_line(source, target, index):
-        @pl.loop(1, NZ)
-        def _(step):
+        for step in LINE_STEPS:
             peer = (z + step) % NZ
             send(source(peer), target.at[z], index, line_peer(peer))
 
@@ -125,9 +136,6 @@
     loads[0].wait()
     loads[1].wait()
     scatter_heads(qk_in, qk, X_QK)
-    loads[2].wait()
-    loads[3].wait()
-    scatter_heads(vg_in, vg, X_VG)
     plane_span = qk.at[:, pl.ds(0, TOK - ROWS), :]
     arrived(plane_span, X_QK)
 
@@ -136,6 +144,9 @@
         mark_out[index] = (summed * (1.0 / SEG)).astype(BF16)
     over_line(lambda peer: mark_out, marks, X_MARK)
     marks[z] = mark_out[...]
+    loads[2].wait()
+    loads[3].wait()
+    scatter_heads(vg_in, vg, X_VG)
     for index in range(2):
         trans[index] = qk[index].T
     arrived(plane_span, X_VG)
@@ -145,6 +156,16 @@
     mark_q = marks[:, 0].reshape(M, HD)
     mark_k = marks[:, 1].reshape(M, HD)
 
+    scores = dot_nt(qk[1], mark_q)
+    key_top = jnp.max(scores, axis=0, keepdims=True)
+    exps = jnp.exp((scores - key_top) * SCALE)
+    kexp[...] = exps
+    key_sum = jnp.sum(exps, axis=0, keepdims=True)
+    stat_out[0:1, :] = key_top
+    stat_out[1:2, :] = key_sum
+    over_line(lambda peer: stat_out, stats, X_STAT)
+    stats[z] = stat_out[...]
+    value_part = dot(trans[2], exps.astype(BF16))
     scores = dot_nt(qk[0], mark_k)
     top = jnp.max(scores, axis=1, keepdims=True)
     exps = jnp.exp((scores - top) * SCALE)
@@ -153,17 +174,8 @@
     token_low = token_prob.astype(BF16)
     low[...] = token_low
     mixing_part = dot(trans[3], token_low)
-
-    scores = dot_nt(qk[1], mark_q)
-    key_top = jnp.max(scores, axis=0, keepdims=True)
-    exps = jnp.exp((scores - key_top) * SCALE)
-    kexp[...] = exps
-    key_sum = jnp.sum(exps, axis=0, keepdims=True)
-    value_part = dot(trans[2], exps.astype(BF16))
-    part_out[:, 0:SLAB, :] = value_part.reshape(NZ, SLAB, M)
-    part_out[:, SLAB : 2 * SLAB, :] = mixing_part.reshape(NZ, SLAB, M)
-    stats = jnp.concatenate([jnp.broadcast_to(key_top, (4, M)), jnp.broadcast_to(key_sum, (4, M))], axis=0)
-    part_out[:, 2 * SLAB : 3 * SLAB, :] = jnp.broadcast_to(stats[None], (NZ, SLAB, M))
+    pair = [value_part.reshape(NZ, SLAB, M), mixing_part.reshape(NZ, SLAB, M)]
+    part_out[...] = jnp.concatenate(pair, axis=1).astype(BF16)
     over_line(lambda peer: part_out.at[peer], parts, X_PART)
     parts[z] = part_out[z]
 
@@ -180,7 +192,6 @@
     def kept(step, slot):
         return saved[step, slot], saved[step, slot + 1]
 
-    mark_split = split(mark_prob)
     keep(ITERS, 8, mark_prob.T)
 
     @pl.loop(0, ITERS)
@@ -200,24 +211,26 @@
 
     keep(ITERS, 0, square[1])
 
+    arrived(stats.at[pl.ds(0, NZ - 1)], X_STAT)
     arrived(parts.at[pl.ds(0, NZ - 1)], X_PART)
-    tops = [parts[peer, 2 * SLAB : 2 * SLAB + 1, :] for peer in range(NZ)]
+    tops = [stats[peer, 0:1, :] for peer in range(NZ)]
     highest = functools.reduce(jnp.maximum, tops)
     total, values, mixing_grad = 0.0, 0.0, 0.0
     for peer in range(NZ):
         weight = jnp.exp((tops[peer] - highest) * SCALE)
-        total = total + weight * parts[peer, 2 * SLAB + 4 : 2 * SLAB + 5, :]
-        values = values + weight * parts[peer, 0:SLAB, :]
-        mixing_grad = mixing_grad + parts[peer, SLAB : 2 * SLAB, :]
-    sum_out[0:SLAB, :] = values / total
-    sum_out[SLAB : 2 * SLAB, :] = mixing_grad
+        total = total + weight * stats[peer, 1:2, :]
+        part = parts[peer].astype(F32)
+        values = values + weight * part[0:SLAB]
+        mixing_grad = mixing_grad + part[SLAB : 2 * SLAB]
+    sum_out[...] = jnp.concatenate([values / total, mixing_grad], axis=0).astype(BF16)
     over_line(lambda peer: sum_out, sums, X_SUM)
     sums[z] = sum_out[...]
     key_prob = kexp[...] * (jnp.exp((key_top - highest) * SCALE) / total)
     kexp[...] = key_prob
     arrived(sums.at[pl.ds(0, NZ - 1)], X_SUM)
-    values = sums[:, 0:SLAB, :].reshape(HD, M)
-    mixing_grad = sums[:, SLAB : 2 * SLAB, :].reshape(HD, M)
+    both = sums[...].astype(F32)
+    values = both[:, 0:SLAB, :].reshape(HD, M)
+    mixing_grad = both[:, SLAB : 2 * SLAB, :].reshape(HD, M)
     values_split, grad_split = split(values), split(mixing_grad)
     inverse = kept(ITERS, 0)
     mixing_low = mul(values_split, inverse, dot_nt).astype(BF16)
@@ -231,35 +244,37 @@
     dots = jnp.sum(token_grad * token_prob, axis=1, keepdims=True)
     token_sgrad = (token_prob * (token_grad - dots)).astype(BF16)
     direct[0] = dot(token_sgrad, mark_k) * SCALE
-    grad_out[0] = (dot(trans[0], token_sgrad) * SCALE).T
+    grad_out[0] = (dot(trans[0], token_sgrad) * SCALE).T.astype(BF16)
     key_prob = kexp[...]
     av_out[1] = dot_nt(key_prob.astype(BF16), lv_low).astype(BF16)
     row_total = jnp.sum(lv_low.astype(F32) * values, axis=0, keepdims=True)
     key_dgrad = dot(vg[0], lv_low)
     key_sgrad = (key_prob * (key_dgrad - row_total)).astype(BF16)
     direct[1] = dot(key_sgrad, mark_q) * SCALE
-    grad_out[1] = (dot(trans[1], key_sgrad) * SCALE).T
+    grad_out[1] = (dot(trans[1], key_sgrad) * SCALE).T.astype(BF16)
     over_line(lambda peer: grad_out.at[:, rows(peer, OWN), :], grads, X_GRAD)
     grads[z] = grad_out[:, rows(z, OWN), :]
     gather_heads(av_out, av_ref, X_AV)
 
+    square[3] = -0.25 * mul(kept(ITERS - 1, 2), split(square[1]))
+
     @pl.loop(0, ITERS)
     def _(back):
         step = ITERS - 1 - back
-        out_grad = square[1]
-        out_split = split(out_grad)
-        second_grad = -0.25 * mul(kept(step, 2), out_split)
-        iterate_grad = 3.25 * out_grad - 0.25 * mul(out_split, kept(step, 8))
+        before = jnp.maximum(step - 1, 0)
+        second_grad = square[3]
         second_split = split(second_grad)
         product_split = kept(step, 4)
-        product_grad = 15.0 * second_grad - mul(second_split, kept(step, 6))
-        first_grad = -mul(product_split, second_split)
-        first_split = split(first_grad)
-        product_grad = product_grad + 7.0 * first_grad
-        product_grad = product_grad - (mul(first_split, product_split) + mul(product_split, first_split))
-        product_grad_split = split(product_grad)
-        square[2] += mul(product_grad_split, kept(step, 0), dot_nt)
-        square[1] = iterate_grad + mul(kept(ITERS, 8), product_grad_split)
+        first_split = kept(step, 6)
+        through = split(mul(product_split, second_split))
+        product_grad = 15.0 * second_grad - (mul(second_split, first_split) + mul(first_split, second_split))
+        product_grad = split(product_grad + mul(through, product_split))
+        out_grad = square[1]
+        out_grad = 3.25 * out_grad - 0.25 * mul(split(out_grad), kept(step, 8))
+        earlier = mul(kept(before, 2), split(out_grad))
+        square[3] = -0.25 * (earlier + mul(kept(before, 4), product_grad))
+        square[1] = out_grad + mul(kept(ITERS, 8), product_grad)
+        square[2] += mul(product_grad, kept(step, 0), dot_nt)
 
     mark_grad = square[2] + square[1].T * factor
     mark_prob = square[0]
@@ -271,8 +286,8 @@
     query_marks = (dot(from_query[0], mark_k) + dot(from_query[1], mark_k)) * SCALE
     key_marks = (dot(from_key[0], mark_q) + dot(from_key[1], mark_q)) * SCALE
     for peer in range(NZ):
-        query_marks = query_marks + grads[peer, 1]
-        key_marks = key_marks + grads[peer, 0]
+        query_marks = query_marks + grads[peer, 1].astype(F32)
+        key_marks = key_marks + grads[peer, 0].astype(F32)
     for index, total in ((0, query_marks), (1, key_marks)):
         spread = direct[index].reshape(OWN, SEG, HD) + (total * (1.0 / SEG))[:, None, :]
         qk_out[index] = spread.reshape(TOK, HD).astype(BF16)
@@ -284,7 +299,7 @@
     for index in (X_QK, X_VG, X_AV, X_OUT):
         left(plane_span, index)
     left(marks.at[pl.ds(0, NZ - 1)], X_MARK)
-    left(parts.at[pl.ds(0, NZ - 1)], X_PART)
+    left(stats.at[pl.ds(0, NZ - 1)], X_STAT); left(parts.at[pl.ds(0, NZ - 1)], X_PART)
     left(sums.at[pl.ds(0, NZ - 1)], X_SUM)
     left(grads.at[pl.ds(0, NZ - 1)], X_GRAD)
 
@@ -304,27 +319,29 @@
             pltpu.VMEM((2, TOK, HD), BF16),
             pltpu.VMEM((2, OWN, HD), BF16),
             pltpu.VMEM((NZ, 2, OWN, HD), BF16),
-            pltpu.VMEM((NZ, 3 * SLAB, M), F32),
-            pltpu.VMEM((NZ, 3 * SLAB, M), F32),
-            pltpu.VMEM((2 * SLAB, M), F32),
-            pltpu.VMEM((NZ, 2 * SLAB, M), F32),
+            pltpu.VMEM((NZ, 2 * SLAB, M), BF16),
+            pltpu.VMEM((NZ, 2 * SLAB, M), BF16),
+            pltpu.VMEM((2, M), F32),
+            pltpu.VMEM((NZ, 2, M), F32),
+            pltpu.VMEM((2 * SLAB, M), BF16),
+            pltpu.VMEM((NZ, 2 * SLAB, M), BF16),
             pltpu.VMEM((2, TOK, HD), BF16),
-            pltpu.VMEM((2, M, HD), F32),
-            pltpu.VMEM((NZ, 2, OWN, HD), F32),
+            pltpu.VMEM((2, M, HD), BF16),
+            pltpu.VMEM((NZ, 2, OWN, HD), BF16),
             pltpu.VMEM((2, TOK, HD), BF16),
             pltpu.VMEM((TOK, M), F32),
             pltpu.VMEM((TOK, M), BF16),
             pltpu.VMEM((TOK, M), F32),
             pltpu.VMEM((4, HD, TOK), BF16),
             pltpu.VMEM((2, TOK, HD), F32),
-            pltpu.VMEM((3, M, M), F32),
+            pltpu.VMEM((4, M, M), F32),
             pltpu.VMEM((ITERS + 1, 10, M, M), BF16),
             pltpu.SemaphoreType.DMA((4,)),
-            pltpu.SemaphoreType.DMA((8,)),
-            pltpu.SemaphoreType.DMA((8,)),
+            pltpu.SemaphoreType.DMA((9,)),
+            pltpu.SemaphoreType.DMA((9,)),
         ],
         compiler_params=pltpu.CompilerParams(
-            collective_id=0, has_side_effects=True, vmem_limit_bytes=48 * 1024 * 1024
+            collective_id=0, has_side_effects=True, vmem_limit_bytes=63 * 1024 * 1024
         ),
     )(queries, keys, values, out_grad)
     return av[0], qk[0], qk[1], av[1]

time: 97.2 us -> 69.4 us (0.71)
  Pallas kernels: 91.9 us -> 66.7 us
  local copies, waits for them, and re-layouts: 4.4 us -> 1.89 us
    pallas_call x1, Pallas kernels: 91.9 us -> 66.7 us  [body(): pl.pallas_call(kernel, out_shape=(pair, pair), in_specs=[anywhere] * 4, o...]
    unnamed x8 -> x0, local copies, waits for them, and re-layouts: 3.61 us -> none
    squeeze x1, local copies, waits for them, and re-layouts: 0.8 us -> 1.89 us  [body(): return (av[0], qk[0], qk[1], av[1])]
where the time goes in v2:
time: 69.4 us; the launch traced here: 69.3 us
  Pallas kernels  66.7 us (96%)
  local copies, waits for them, and re-layouts  1.89 us (3%)
    pallas_call x1, Pallas kernels, body(): pl.pallas_call(kernel, out_shape=(pair, pair), in_specs=[anywhere] * 4, o...  66.7 us
    squeeze x1, local copies, waits for them, and re-layouts, body(): return (av[0], qk[0], qk[1], av[1])  1.89 us

profile of v2, /device:TPU:1, one launch (start us, length us, event | category | flops | bytes accessed | tf_op | source)
XLA Modules:
  0.0 69.3 jit_solution(8905719622756227259)
XLA Ops:
  0.6 66.7 %shard_map.75 = (bf16[2,16,4096]{2,1,0:T(8,128)(2,1)}, bf16[2,16,4096]{2,1,0:T(8,128)(2,1)}) custom-call(bf16[16,4096]{1,0:T(8,128)(2,1)} %q_ref.1, bf16[16,4096]{1,0:T(8,128)(2,1)} %k_ref.1, bf16[16,4096]{1,0:T(8,128)(2,1)} %v_ref.1, bf16[16,4096]{1,0:T(8,128)(2,1)} %g_ref.1), custom_call_target="tpu_custom_call" | custom-call | tf_op jit(solution)/shard_map/pallas_call | solution.py:310
  67.4 1.9 %slice_bitcast_fusion = (bf16[16,4096]{1,0:T(8,128)(2,1)}, bf16[16,4096]{1,0:T(8,128)(2,1)}, bf16[16,4096]{1,0:T(8,128)(2,1)}, bf16[16,4096]{1,0:T(8,128)(2,1)}) fusion(bf16[2,16,4096]{2,1,0:T(8,128)(2,1)} %get-tuple-element.6, bf16[2,16,4096]{2,1,0:T(8,128)(2,1)} %get-tuple-element.7), kind=kLoop, calls=%fused_computation | loop fusion | bytes 1048576 | tf_op jit(solution)/shard_map/squeeze | solution.py:347

commit v3 on v2

--- a/solution.py
+++ b/solution.py
@@ -34,6 +34,7 @@
     ((i, j, k) for i in range(NY) for j in range(NX) for k in range(2) if i or j or k),
     key=lambda step: -away(step[0], NY) - away(step[1], NX),
 )
+CHIP_STEPS = [(i, j) for i, j, k in PLANE_STEPS if k == 0]
 LINE_STEPS = sorted(range(1, NZ), key=lambda step: -away(step, NZ))
 
 X_QK, X_VG, X_MARK, X_PART, X_SUM, X_AV, X_GRAD, X_OUT, X_STAT = range(9)
@@ -59,7 +60,7 @@
 def kernel(
     q_ref, k_ref, v_ref, g_ref, av_ref, qk_ref,
     qk_in, vg_in, qk, vg, mark_out, marks, part_out, parts, stat_out, stats, sum_out, sums, av_out, grad_out, grads, qk_out,
-    prob, low, kexp, trans, direct, square, saved, load_sem, send_sem, recv_sem,
+    prob, low, kexp, trans, direct, square, saved, sync_sem, load_sem, send_sem, recv_sem,
 ):
     seq, head = lax.axis_index("seq"), lax.axis_index("head")
     y, z = seq // NZ, seq % NZ
@@ -81,16 +82,29 @@
         load.start()
 
     barrier = pltpu.get_barrier_semaphore()
-
-    @pl.loop(1, PLANE)
-    def _(step):
-        pl.semaphore_signal(barrier, inc=1, device_id=plane_peer((me + step) % PLANE), device_id_type=MESH)
-
-    @pl.loop(1, NZ)
-    def _(step):
-        pl.semaphore_signal(barrier, inc=1, device_id=line_peer((z + step) % NZ), device_id_type=MESH)
-
-    pl.semaphore_wait(barrier, PLANE - 1 + NZ - 1)
+    core, x = head % 2, head // 2
+    sibling = (seq, head + 1 - 2 * core)
+
+    def greet(peer):
+        pl.semaphore_signal(barrier, inc=1, device_id=peer, device_id_type=MESH)
+
+    for i, j in CHIP_STEPS:
+        greet(((y + i) % NY * NZ + z, (x + j) % NX * 2))
+    greet(sibling)
+    for step in LINE_STEPS:
+        greet((y * NZ + (z + step) % NZ, 2 * x + 1))
+
+    def met(first):
+        @pl.when(core == first)
+        def _():
+            pl.semaphore_wait(barrier, PLANE - 1)
+            pl.semaphore_signal(sync_sem, inc=1, device_id=sibling, device_id_type=MESH)
+
+        @pl.when(core != first)
+        def _():
+            pl.semaphore_wait(sync_sem, 1)
+
+    met(0)
 
     def send(source, target, index, peer):
         pltpu.make_async_remote_copy(
@@ -114,13 +128,13 @@
 
         target[:, rows(me, ROWS), :] = source[:, :, columns(me)]
 
-    def gather_heads(source, target, index):
-        for peer in plane_ranks():
-            send(source.at[:, rows(peer, ROWS), :], target.at[:, :, columns(me)], index, plane_peer(peer))
-
-        own = pltpu.make_async_copy(source.at[:, rows(me, ROWS), :], target.at[:, :, columns(me)], load_sem.at[0])
-        own.start()
-        own.wait()
+    def return_to(peer, source, target, index):
+        send(source.at[:, rows(peer, ROWS), :], target.at[:, :, columns(me)], index, plane_peer(peer))
+
+    def own_block(source, target, index):
+        return pltpu.make_async_copy(
+            source.at[:, rows(me, ROWS), :], target.at[:, :, columns(me)], load_sem.at[index]
+        )
 
     def over_line(source, target, index):
         for step in LINE_STEPS:
@@ -142,6 +156,7 @@
     for index in range(2):
         summed = jnp.sum(qk[index].astype(F32).reshape(OWN, SEG, HD), axis=1)
         mark_out[index] = (summed * (1.0 / SEG)).astype(BF16)
+    met(1)
     over_line(lambda peer: mark_out, marks, X_MARK)
     marks[z] = mark_out[...]
     loads[2].wait()
@@ -212,20 +227,21 @@
     keep(ITERS, 0, square[1])
 
     arrived(stats.at[pl.ds(0, NZ - 1)], X_STAT)
-    arrived(parts.at[pl.ds(0, NZ - 1)], X_PART)
     tops = [stats[peer, 0:1, :] for peer in range(NZ)]
     highest = functools.reduce(jnp.maximum, tops)
-    total, values, mixing_grad = 0.0, 0.0, 0.0
+    weights = [jnp.exp((top - highest) * SCALE) for top in tops]
+    total = sum(weight * stats[peer, 1:2, :] for peer, weight in enumerate(weights))
+    inverse_total = 1.0 / total
+    arrived(parts.at[pl.ds(0, NZ - 1)], X_PART)
+    values, mixing_grad = 0.0, 0.0
     for peer in range(NZ):
-        weight = jnp.exp((tops[peer] - highest) * SCALE)
-        total = total + weight * stats[peer, 1:2, :]
         part = parts[peer].astype(F32)
-        values = values + weight * part[0:SLAB]
+        values = values + weights[peer] * part[0:SLAB]
         mixing_grad = mixing_grad + part[SLAB : 2 * SLAB]
-    sum_out[...] = jnp.concatenate([values / total, mixing_grad], axis=0).astype(BF16)
+    sum_out[...] = jnp.concatenate([values * inverse_total, mixing_grad], axis=0).astype(BF16)
     over_line(lambda peer: sum_out, sums, X_SUM)
     sums[z] = sum_out[...]
-    key_prob = kexp[...] * (jnp.exp((key_top - highest) * SCALE) / total)
+    key_prob = kexp[...] * (jnp.exp((key_top - highest) * SCALE) * inverse_total)
     kexp[...] = key_prob
     arrived(sums.at[pl.ds(0, NZ - 1)], X_SUM)
     both = sums[...].astype(F32)
@@ -254,14 +270,12 @@
     grad_out[1] = (dot(trans[1], key_sgrad) * SCALE).T.astype(BF16)
     over_line(lambda peer: grad_out.at[:, rows(peer, OWN), :], grads, X_GRAD)
     grads[z] = grad_out[:, rows(z, OWN), :]
-    gather_heads(av_out, av_ref, X_AV)
+    own_block(av_out, av_ref, 0).start()
+    return_to((me + PLANE - 1) % PLANE, av_out, av_ref, X_AV)
 
     square[3] = -0.25 * mul(kept(ITERS - 1, 2), split(square[1]))
 
-    @pl.loop(0, ITERS)
-    def _(back):
-        step = ITERS - 1 - back
-        before = jnp.maximum(step - 1, 0)
+    def step_back(step, before):
         second_grad = square[3]
         second_split = split(second_grad)
         product_split = kept(step, 4)
@@ -275,6 +289,15 @@
         square[3] = -0.25 * (earlier + mul(kept(before, 4), product_grad))
         square[1] = out_grad + mul(kept(ITERS, 8), product_grad)
         square[2] += mul(product_grad, kept(step, 0), dot_nt)
+
+    step_back(ITERS - 1, ITERS - 2)
+
+    @pl.loop(1, ITERS)
+    def _(back):
+        for turn in range(6):
+            return_to((me + 1 + (back - 1) * 6 + turn) % PLANE, av_out, av_ref, X_AV)
+        step = ITERS - 1 - back
+        step_back(step, jnp.maximum(step - 1, 0))
 
     mark_grad = square[2] + square[1].T * factor
     mark_prob = square[0]
@@ -291,9 +314,13 @@
     for index, total in ((0, query_marks), (1, key_marks)):
         spread = direct[index].reshape(OWN, SEG, HD) + (total * (1.0 / SEG))[:, None, :]
         qk_out[index] = spread.reshape(TOK, HD).astype(BF16)
-    gather_heads(qk_out, qk_ref, X_OUT)
+    for peer in plane_ranks():
+        return_to(peer, qk_out, qk_ref, X_OUT)
+    own_block(qk_out, qk_ref, 1).start()
 
     out_span = av_ref.at[:, :, pl.ds(0, D - HD)]
+    own_block(av_out, av_ref, 0).wait()
+    own_block(qk_out, qk_ref, 1).wait()
     arrived(out_span, X_AV)
     arrived(out_span, X_OUT)
     for index in (X_QK, X_VG, X_AV, X_OUT):
@@ -336,6 +363,7 @@
             pltpu.VMEM((2, TOK, HD), F32),
             pltpu.VMEM((4, M, M), F32),
             pltpu.VMEM((ITERS + 1, 10, M, M), BF16),
+            pltpu.SemaphoreType.REGULAR,
             pltpu.SemaphoreType.DMA((4,)),
             pltpu.SemaphoreType.DMA((9,)),
             pltpu.SemaphoreType.DMA((9,)),

time: 69.4 us -> 66.6 us (0.960)
  Pallas kernels: 66.7 us -> 63.9 us
    pallas_call x1, Pallas kernels: 66.7 us -> 63.9 us  [body(): pl.pallas_call(kernel, out_shape=(pair, pair), in_specs=[anywhere] * 4, o...]
where the time goes in v3:
time: 66.6 us; the launch traced here: 66.4 us
  Pallas kernels  63.9 us (96%)
  local copies, waits for them, and re-layouts  1.89 us (3%)
    pallas_call x1, Pallas kernels, body(): pl.pallas_call(kernel, out_shape=(pair, pair), in_specs=[anywhere] * 4, o...  63.9 us
    squeeze x1, local copies, waits for them, and re-layouts, body(): return (av[0], qk[0], qk[1], av[1])  1.89 us

profile of v3, /device:TPU:1, one launch (start us, length us, event | category | flops | bytes accessed | tf_op | source)
XLA Modules:
  0.0 66.4 jit_solution(10078285697639836705)
XLA Ops:
  0.6 63.9 %shard_map.75 = (bf16[2,16,4096]{2,1,0:T(8,128)(2,1)}, bf16[2,16,4096]{2,1,0:T(8,128)(2,1)}) custom-call(bf16[16,4096]{1,0:T(8,128)(2,1)} %q_ref.1, bf16[16,4096]{1,0:T(8,128)(2,1)} %k_ref.1, bf16[16,4096]{1,0:T(8,128)(2,1)} %v_ref.1, bf16[16,4096]{1,0:T(8,128)(2,1)} %g_ref.1), custom_call_target="tpu_custom_call" | custom-call | tf_op jit(solution)/shard_map/pallas_call | solution.py:337
  64.5 1.9 %slice_bitcast_fusion = (bf16[16,4096]{1,0:T(8,128)(2,1)}, bf16[16,4096]{1,0:T(8,128)(2,1)}, bf16[16,4096]{1,0:T(8,128)(2,1)}, bf16[16,4096]{1,0:T(8,128)(2,1)}) fusion(bf16[2,16,4096]{2,1,0:T(8,128)(2,1)} %get-tuple-element.6, bf16[2,16,4096]{2,1,0:T(8,128)(2,1)} %get-tuple-element.7), kind=kLoop, calls=%fused_computation | loop fusion | bytes 1048576 | tf_op jit(solution)/shard_map/squeeze | solution.py:375

commit v4 on v3

--- a/solution.py
+++ b/solution.py
@@ -57,6 +57,14 @@
     return product(left[0], right[0]) + (product(left[0], right[1]) + product(left[1], right[0]))
 
 
+def mul_left(left, right, product=dot):
+    return product(left, right[0]) + product(left, right[1])
+
+
+def mul_right(left, right):
+    return dot(left[0], right) + dot(left[1], right)
+
+
 def kernel(
     q_ref, k_ref, v_ref, g_ref, av_ref, qk_ref,
     qk_in, vg_in, qk, vg, mark_out, marks, part_out, parts, stat_out, stats, sum_out, sums, av_out, grad_out, grads, qk_out,
@@ -164,9 +172,6 @@
     scatter_heads(vg_in, vg, X_VG)
     for index in range(2):
         trans[index] = qk[index].T
-    arrived(plane_span, X_VG)
-    for index in range(2):
-        trans[2 + index] = vg[index].T
     arrived(marks.at[pl.ds(0, NZ - 1)], X_MARK)
     mark_q = marks[:, 0].reshape(M, HD)
     mark_k = marks[:, 1].reshape(M, HD)
@@ -180,6 +185,9 @@
     stat_out[1:2, :] = key_sum
     over_line(lambda peer: stat_out, stats, X_STAT)
     stats[z] = stat_out[...]
+    arrived(plane_span, X_VG)
+    for index in range(2):
+        trans[2 + index] = vg[index].T
     value_part = dot(trans[2], exps.astype(BF16))
     scores = dot_nt(qk[0], mark_k)
     top = jnp.max(scores, axis=1, keepdims=True)
@@ -246,12 +254,11 @@
     arrived(sums.at[pl.ds(0, NZ - 1)], X_SUM)
     both = sums[...].astype(F32)
     values = both[:, 0:SLAB, :].reshape(HD, M)
-    mixing_grad = both[:, SLAB : 2 * SLAB, :].reshape(HD, M)
-    values_split, grad_split = split(values), split(mixing_grad)
+    values_low, mixing_grad = values.astype(BF16), both[:, SLAB : 2 * SLAB, :].reshape(HD, M).astype(BF16)
     inverse = kept(ITERS, 0)
-    mixing_low = mul(values_split, inverse, dot_nt).astype(BF16)
-    lv_low = mul(grad_split, inverse).astype(BF16)
-    square[1] = mul(split(mixing_grad.T), values_split)
+    square[1] = dot(mixing_grad.T, values_low)
+    mixing_low = (mul_left(values_low, inverse, dot_nt)).astype(BF16)
+    lv_low = (mul_left(mixing_grad, inverse)).astype(BF16)
     square[2] = jnp.zeros((M, M), F32)
 
     token_prob = prob[...]
@@ -271,33 +278,36 @@
     over_line(lambda peer: grad_out.at[:, rows(peer, OWN), :], grads, X_GRAD)
     grads[z] = grad_out[:, rows(z, OWN), :]
     own_block(av_out, av_ref, 0).start()
-    return_to((me + PLANE - 1) % PLANE, av_out, av_ref, X_AV)
-
-    square[3] = -0.25 * mul(kept(ITERS - 1, 2), split(square[1]))
+
+    square[3] = -0.25 * mul_right(kept(ITERS - 1, 2), square[1].astype(BF16))
 
     def step_back(step, before):
         second_grad = square[3]
-        second_split = split(second_grad)
+        second_low = second_grad.astype(BF16)
         product_split = kept(step, 4)
         first_split = kept(step, 6)
-        through = split(mul(product_split, second_split))
-        product_grad = 15.0 * second_grad - (mul(second_split, first_split) + mul(first_split, second_split))
-        product_grad = split(product_grad + mul(through, product_split))
+        through = mul_right(product_split, second_low).astype(BF16)
+        product_grad = 15.0 * second_grad - (mul_left(second_low, first_split) + mul_right(first_split, second_low))
+        product_grad = (product_grad + mul_left(through, product_split)).astype(BF16)
         out_grad = square[1]
-        out_grad = 3.25 * out_grad - 0.25 * mul(split(out_grad), kept(step, 8))
-        earlier = mul(kept(before, 2), split(out_grad))
-        square[3] = -0.25 * (earlier + mul(kept(before, 4), product_grad))
-        square[1] = out_grad + mul(kept(ITERS, 8), product_grad)
-        square[2] += mul(product_grad, kept(step, 0), dot_nt)
+        out_grad = 3.25 * out_grad - 0.25 * mul_left(out_grad.astype(BF16), kept(step, 8))
+        if before is not None:
+            earlier = mul_right(kept(before, 2), out_grad.astype(BF16))
+            square[3] = -0.25 * (earlier + mul_right(kept(before, 4), product_grad))
+        square[1] = out_grad + mul_right(kept(ITERS, 8), product_grad)
+        square[2] += mul_left(product_grad, kept(step, 0), dot_nt)
 
     step_back(ITERS - 1, ITERS - 2)
-
-    @pl.loop(1, ITERS)
+    for turn in range(3):
+        return_to((me + 1 + turn) % PLANE, av_out, av_ref, X_AV)
+
+    @pl.loop(1, ITERS - 1)
     def _(back):
-        for turn in range(6):
-            return_to((me + 1 + (back - 1) * 6 + turn) % PLANE, av_out, av_ref, X_AV)
-        step = ITERS - 1 - back
-        step_back(step, jnp.maximum(step - 1, 0))
+        for turn in range(7):
+            return_to((me + 4 + (back - 1) * 7 + turn) % PLANE, av_out, av_ref, X_AV)
+        step_back(ITERS - 1 - back, ITERS - 2 - back)
+
+    step_back(0, None)
 
     mark_grad = square[2] + square[1].T * factor
     mark_prob = square[0]

time: 66.6 us -> 65.2 us (0.979)
  Pallas kernels: 63.9 us -> 62.5 us
    pallas_call x1, Pallas kernels: 63.9 us -> 62.5 us  [body(): pl.pallas_call(kernel, out_shape=(pair, pair), in_specs=[anywhere] * 4, o...]
where the time goes in v4:
time: 65.2 us; the launch traced here: 65 us
  Pallas kernels  62.5 us (96%)
  local copies, waits for them, and re-layouts  1.89 us (3%)
    pallas_call x1, Pallas kernels, body(): pl.pallas_call(kernel, out_shape=(pair, pair), in_specs=[anywhere] * 4, o...  62.5 us
    squeeze x1, local copies, waits for them, and re-layouts, body(): return (av[0], qk[0], qk[1], av[1])  1.89 us

profile of v4, /device:TPU:1, one launch (start us, length us, event | category | flops | bytes accessed | tf_op | source)
XLA Modules:
  0.0 65.0 jit_solution(8559875377017057454)
XLA Ops:
  0.6 62.5 %shard_map.75 = (bf16[2,16,4096]{2,1,0:T(8,128)(2,1)}, bf16[2,16,4096]{2,1,0:T(8,128)(2,1)}) custom-call(bf16[16,4096]{1,0:T(8,128)(2,1)} %q_ref.1, bf16[16,4096]{1,0:T(8,128)(2,1)} %k_ref.1, bf16[16,4096]{1,0:T(8,128)(2,1)} %v_ref.1, bf16[16,4096]{1,0:T(8,128)(2,1)} %g_ref.1), custom_call_target="tpu_custom_call" | custom-call | tf_op jit(solution)/shard_map/pallas_call | solution.py:347
  63.1 1.9 %slice_bitcast_fusion = (bf16[16,4096]{1,0:T(8,128)(2,1)}, bf16[16,4096]{1,0:T(8,128)(2,1)}, bf16[16,4096]{1,0:T(8,128)(2,1)}, bf16[16,4096]{1,0:T(8,128)(2,1)}) fusion(bf16[2,16,4096]{2,1,0:T(8,128)(2,1)} %get-tuple-element.6, bf16[2,16,4096]{2,1,0:T(8,128)(2,1)} %get-tuple-element.7), kind=kLoop, calls=%fused_computation | loop fusion | bytes 1048576 | tf_op jit(solution)/shard_map/squeeze | solution.py:385

commit v5 on v4

--- a/solution.py
+++ b/solution.py
@@ -37,7 +37,7 @@
 CHIP_STEPS = [(i, j) for i, j, k in PLANE_STEPS if k == 0]
 LINE_STEPS = sorted(range(1, NZ), key=lambda step: -away(step, NZ))
 
-X_QK, X_VG, X_MARK, X_PART, X_SUM, X_AV, X_GRAD, X_OUT, X_STAT = range(9)
+X_QK, X_VG, X_MARK, X_PART, X_SUM, X_AV, X_GRAD, X_OUT, X_STAT, X_GRAD_B = range(10)
 
 
 def dot(left, right):
@@ -267,16 +267,18 @@
     dots = jnp.sum(token_grad * token_prob, axis=1, keepdims=True)
     token_sgrad = (token_prob * (token_grad - dots)).astype(BF16)
     direct[0] = dot(token_sgrad, mark_k) * SCALE
-    grad_out[0] = (dot(trans[0], token_sgrad) * SCALE).T.astype(BF16)
+    grad_out[0] = (dot(trans[0], token_sgrad) * SCALE).astype(BF16).T
+    over_line(lambda peer: grad_out.at[0, rows(peer, OWN), :], grads.at[0], X_GRAD)
     key_prob = kexp[...]
     av_out[1] = dot_nt(key_prob.astype(BF16), lv_low).astype(BF16)
     row_total = jnp.sum(lv_low.astype(F32) * values, axis=0, keepdims=True)
     key_dgrad = dot(vg[0], lv_low)
     key_sgrad = (key_prob * (key_dgrad - row_total)).astype(BF16)
     direct[1] = dot(key_sgrad, mark_q) * SCALE
-    grad_out[1] = (dot(trans[1], key_sgrad) * SCALE).T.astype(BF16)
-    over_line(lambda peer: grad_out.at[:, rows(peer, OWN), :], grads, X_GRAD)
-    grads[z] = grad_out[:, rows(z, OWN), :]
+    grad_out[1] = (dot(trans[1], key_sgrad) * SCALE).astype(BF16).T
+    over_line(lambda peer: grad_out.at[1, rows(peer, OWN), :], grads.at[1], X_GRAD_B)
+    for index in range(2):
+        grads[index, z] = grad_out[index, rows(z, OWN), :]
     own_block(av_out, av_ref, 0).start()
 
     square[3] = -0.25 * mul_right(kept(ITERS - 1, 2), square[1].astype(BF16))
@@ -314,13 +316,15 @@
     mark_sgrad = mark_prob * (mark_grad - jnp.sum(mark_grad * mark_prob, axis=1, keepdims=True))
     square[1] = mark_sgrad
     square[2] = mark_sgrad.T
-    arrived(grads.at[pl.ds(0, NZ - 1)], X_GRAD)
+    grad_span = grads.at[0, pl.ds(0, NZ - 1)]
+    arrived(grad_span, X_GRAD)
+    arrived(grad_span, X_GRAD_B)
     from_query, from_key = split(square[1, rows(z, OWN), :]), split(square[2, rows(z, OWN), :])
     query_marks = (dot(from_query[0], mark_k) + dot(from_query[1], mark_k)) * SCALE
     key_marks = (dot(from_key[0], mark_q) + dot(from_key[1], mark_q)) * SCALE
     for peer in range(NZ):
-        query_marks = query_marks + grads[peer, 1].astype(F32)
-        key_marks = key_marks + grads[peer, 0].astype(F32)
+        query_marks = query_marks + grads[1, peer].astype(F32)
+        key_marks = key_marks + grads[0, peer].astype(F32)
     for index, total in ((0, query_marks), (1, key_marks)):
         spread = direct[index].reshape(OWN, SEG, HD) + (total * (1.0 / SEG))[:, None, :]
         qk_out[index] = spread.reshape(TOK, HD).astype(BF16)
@@ -338,7 +342,8 @@
     left(marks.at[pl.ds(0, NZ - 1)], X_MARK)
     left(stats.at[pl.ds(0, NZ - 1)], X_STAT); left(parts.at[pl.ds(0, NZ - 1)], X_PART)
     left(sums.at[pl.ds(0, NZ - 1)], X_SUM)
-    left(grads.at[pl.ds(0, NZ - 1)], X_GRAD)
+    left(grad_span, X_GRAD)
+    left(grad_span, X_GRAD_B)
 
 
 def body(queries, keys, values, out_grad):
@@ -364,7 +369,7 @@
             pltpu.VMEM((NZ, 2 * SLAB, M), BF16),
             pltpu.VMEM((2, TOK, HD), BF16),
             pltpu.VMEM((2, M, HD), BF16),
-            pltpu.VMEM((NZ, 2, OWN, HD), BF16),
+            pltpu.VMEM((2, NZ, OWN, HD), BF16),
             pltpu.VMEM((2, TOK, HD), BF16),
             pltpu.VMEM((TOK, M), F32),
             pltpu.VMEM((TOK, M), BF16),
@@ -375,8 +380,8 @@
             pltpu.VMEM((ITERS + 1, 10, M, M), BF16),
             pltpu.SemaphoreType.REGULAR,
             pltpu.SemaphoreType.DMA((4,)),
-            pltpu.SemaphoreType.DMA((9,)),
-            pltpu.SemaphoreType.DMA((9,)),
+            pltpu.SemaphoreType.DMA((10,)),
+            pltpu.SemaphoreType.DMA((10,)),
         ],
         compiler_params=pltpu.CompilerParams(
             collective_id=0, has_side_effects=True, vmem_limit_bytes=63 * 1024 * 1024

time: 65.2 us -> 65.2 us (level)
  no operation moved by 1% of the time
where the time goes in v5:
time: 65.2 us; the launch traced here: 65.1 us
  Pallas kernels  62.6 us (96%)
  local copies, waits for them, and re-layouts  1.89 us (3%)
    pallas_call x1, Pallas kernels, body(): pl.pallas_call(kernel, out_shape=(pair, pair), in_specs=[anywhere] * 4, o...  62.6 us
    squeeze x1, local copies, waits for them, and re-layouts, body(): return (av[0], qk[0], qk[1], av[1])  1.89 us

profile of v5, /device:TPU:1, one launch (start us, length us, event | category | flops | bytes accessed | tf_op | source)
XLA Modules:
  0.0 65.1 jit_solution(5544091377852159235)
XLA Ops:
  0.6 62.6 %shard_map.75 = (bf16[2,16,4096]{2,1,0:T(8,128)(2,1)}, bf16[2,16,4096]{2,1,0:T(8,128)(2,1)}) custom-call(bf16[16,4096]{1,0:T(8,128)(2,1)} %q_ref.1, bf16[16,4096]{1,0:T(8,128)(2,1)} %k_ref.1, bf16[16,4096]{1,0:T(8,128)(2,1)} %v_ref.1, bf16[16,4096]{1,0:T(8,128)(2,1)} %g_ref.1), custom_call_target="tpu_custom_call" | custom-call | tf_op jit(solution)/shard_map/pallas_call | solution.py:352
  63.2 1.9 %slice_bitcast_fusion = (bf16[16,4096]{1,0:T(8,128)(2,1)}, bf16[16,4096]{1,0:T(8,128)(2,1)}, bf16[16,4096]{1,0:T(8,128)(2,1)}, bf16[16,4096]{1,0:T(8,128)(2,1)}) fusion(bf16[2,16,4096]{2,1,0:T(8,128)(2,1)} %get-tuple-element.6, bf16[2,16,4096]{2,1,0:T(8,128)(2,1)} %get-tuple-element.7), kind=kLoop, calls=%fused_computation | loop fusion | bytes 1048576 | tf_op jit(solution)/shard_map/squeeze | solution.py:390

commit v6 on v5

--- a/solution.py
+++ b/solution.py
@@ -256,7 +256,6 @@
     values = both[:, 0:SLAB, :].reshape(HD, M)
     values_low, mixing_grad = values.astype(BF16), both[:, SLAB : 2 * SLAB, :].reshape(HD, M).astype(BF16)
     inverse = kept(ITERS, 0)
-    square[1] = dot(mixing_grad.T, values_low)
     mixing_low = (mul_left(values_low, inverse, dot_nt)).astype(BF16)
     lv_low = (mul_left(mixing_grad, inverse)).astype(BF16)
     square[2] = jnp.zeros((M, M), F32)
@@ -281,6 +280,7 @@
         grads[index, z] = grad_out[index, rows(z, OWN), :]
     own_block(av_out, av_ref, 0).start()
 
+    square[1] = dot(mixing_grad.T, values_low)
     square[3] = -0.25 * mul_right(kept(ITERS - 1, 2), square[1].astype(BF16))
 
     def step_back(step, before):

time: 65.2 us -> 65.2 us (level)
  no operation moved by 1% of the time
where the time goes in v6:
time: 65.2 us; the launch traced here: 65.1 us
  Pallas kernels  62.6 us (96%)
  local copies, waits for them, and re-layouts  1.89 us (3%)
    pallas_call x1, Pallas kernels, body(): pl.pallas_call(kernel, out_shape=(pair, pair), in_specs=[anywhere] * 4, o...  62.6 us
    squeeze x1, local copies, waits for them, and re-layouts, body(): return (av[0], qk[0], qk[1], av[1])  1.89 us

profile of v6, /device:TPU:1, one launch (start us, length us, event | category | flops | bytes accessed | tf_op | source)
XLA Modules:
  0.0 65.1 jit_solution(10372192253778487132)
XLA Ops:
  0.6 62.6 %shard_map.75 = (bf16[2,16,4096]{2,1,0:T(8,128)(2,1)}, bf16[2,16,4096]{2,1,0:T(8,128)(2,1)}) custom-call(bf16[16,4096]{1,0:T(8,128)(2,1)} %q_ref.1, bf16[16,4096]{1,0:T(8,128)(2,1)} %k_ref.1, bf16[16,4096]{1,0:T(8,128)(2,1)} %v_ref.1, bf16[16,4096]{1,0:T(8,128)(2,1)} %g_ref.1), custom_call_target="tpu_custom_call" | custom-call | tf_op jit(solution)/shard_map/pallas_call | solution.py:352
  63.2 1.9 %slice_bitcast_fusion = (bf16[16,4096]{1,0:T(8,128)(2,1)}, bf16[16,4096]{1,0:T(8,128)(2,1)}, bf16[16,4096]{1,0:T(8,128)(2,1)}, bf16[16,4096]{1,0:T(8,128)(2,1)}) fusion(bf16[2,16,4096]{2,1,0:T(8,128)(2,1)} %get-tuple-element.6, bf16[2,16,4096]{2,1,0:T(8,128)(2,1)} %get-tuple-element.7), kind=kLoop, calls=%fused_computation | loop fusion | bytes 1048576 | tf_op jit(solution)/shard_map/squeeze | solution.py:390
